TPU v7x, 32 devices: a whole 2x2x4 slice. The times are simulated.
32 devices in a mesh: seq: 8 (over z, y), ch: 4 (over x, core).
Axes of the slice: x: 2, y: 2, z: 4, core: 2. Of those that a mesh axis runs over, the one named last changes fastest.
Arguments:
- query_rows: bfloat16 [2048, 4096], P(('seq', 'ch')), may hold values from -6 to 6
- key_rows: bfloat16 [2048, 4096], P(('seq', 'ch')), may hold values from -6 to 6
- value_rows: bfloat16 [2048, 4096], P(('seq', 'ch')), may hold values from -6 to 6
- filter_taps: float32 [2048, 4096], P(('seq', 'ch')), may hold values from -1.1 to 1.1
- skip_gain: float32 [4096], replicated, may hold values from 0.5 to 1.5
Outputs:
- gated_output: bfloat16 [2048, 4096], P(('seq', 'ch'))
All inputs are finite; a program needn't handle non-finite values.
Results may differ from a plain program's by a relative error of at most 0.0014.
Values sent between devices are 32-bit elements; how exact they have to be, the bound alone decides.
A program may use at most 128 MiB of HBM per device.

v0:
```python
import math
import jax
import jax.numpy as jnp
from jax import lax
from jax.sharding import PartitionSpec as P

highest = lax.Precision.HIGHEST


def angles(product_ids, modulus):
    return 2.0 * math.pi / modulus * (product_ids % modulus).astype(jnp.float32)


def contract(pattern, weights, operand):
    return jnp.einsum(
        pattern, weights, operand, precision=highest, preferred_element_type=jnp.float32
    )


def shards(query_rows, key_rows, value_rows, filter_taps, skip_gain):
    seq_count = lax.axis_size("seq")
    group_count = lax.axis_size("ch")
    position = lax.axis_index("seq")
    row_count, full_width = key_rows.shape
    per_peer = row_count // seq_count
    columns = full_width // group_count
    local_rows = group_count * per_peer
    tokens = row_count * group_count
    slot_count = 2 * seq_count
    length = 2 * tokens * seq_count
    signal = key_rows.astype(jnp.float32) * value_rows.astype(jnp.float32)
    layout = (1, seq_count, 1, per_peer, full_width)
    moved_signal, moved_filter = (
        lax.all_to_all(
            lax.all_to_all(signal.reshape(layout), "seq", split_axis=1, concat_axis=0, tiled=True),
            "ch",
            split_axis=4,
            concat_axis=2,
            tiled=True,
        ),
        lax.all_to_all(
            lax.all_to_all(
                filter_taps.reshape(layout), "seq", split_axis=1, concat_axis=0, tiled=True
            ),
            "ch",
            split_axis=4,
            concat_axis=2,
            tiled=True,
        ),
    )
    moved_signal = moved_signal.reshape(seq_count, local_rows, columns)
    moved_filter = moved_filter.reshape(seq_count, local_rows, columns)
    slot_ids = jnp.arange(slot_count, dtype=jnp.int32)
    owners = slot_ids // 2
    freq_slot = jnp.where(
        slot_ids % 2 == 0, owners, jnp.where(owners == 0, seq_count, slot_count - owners)
    )
    blocks = jnp.arange(seq_count, dtype=jnp.int32)
    block_phase = angles(freq_slot[:, None] * blocks[None, :], slot_count)
    block_cos = jnp.cos(block_phase)
    block_sin = jnp.sin(block_phase)
    local_ids = jnp.arange(local_rows, dtype=jnp.int32)
    local_time = local_ids // per_peer * row_count + position * per_peer + local_ids % per_peer
    twist_angle = -angles(freq_slot[:, None] * local_time[None, :], length)
    twist_cos = jnp.cos(twist_angle)[:, :, None]
    twist_sin = jnp.sin(twist_angle)[:, :, None]

    def forward_blocks(real_part):
        out_real = contract("jd,dmc->jmc", block_cos, real_part)
        out_imag = -contract("jd,dmc->jmc", block_sin, real_part)
        return jnp.stack(
            [
                out_real * twist_cos - out_imag * twist_sin,
                out_real * twist_sin + out_imag * twist_cos,
            ]
        )

    all_ids = jnp.arange(tokens, dtype=jnp.int32)
    peer_id = all_ids // local_rows
    within = all_ids % local_rows
    all_time = within // per_peer * row_count + peer_id * per_peer + within % per_peer
    inner_phase = angles(all_ids[:, None] * all_time[None, :], tokens)
    inner_cos = jnp.cos(inner_phase)
    inner_sin = jnp.sin(inner_phase)

    def forward_inner(spectrum):
        real_part = spectrum[0]
        imag_part = spectrum[1]
        out_real = contract("qp,jpc->jqc", inner_cos, real_part) + contract(
            "qp,jpc->jqc", inner_sin, imag_part
        )
        out_imag = contract("qp,jpc->jqc", inner_cos, imag_part) - contract(
            "qp,jpc->jqc", inner_sin, real_part
        )
        return (out_real, out_imag)

    signal_spectrum, filter_spectrum = (
        lax.all_to_all(
            forward_blocks(moved_signal), "seq", split_axis=1, concat_axis=2, tiled=True
        ),
        lax.all_to_all(
            forward_blocks(moved_filter), "seq", split_axis=1, concat_axis=2, tiled=True
        ),
    )
    signal_real, signal_imag = forward_inner(signal_spectrum)
    filter_real, filter_imag = forward_inner(filter_spectrum)
    product_real = signal_real * filter_real - signal_imag * filter_imag
    product_imag = signal_real * filter_imag + signal_imag * filter_real
    back_real = contract("qp,jqc->jpc", inner_cos, product_real) - contract(
        "qp,jqc->jpc", inner_sin, product_imag
    )
    back_imag = contract("qp,jqc->jpc", inner_cos, product_imag) + contract(
        "qp,jqc->jpc", inner_sin, product_real
    )
    my_slots = jnp.stack([position, jnp.where(position == 0, seq_count, slot_count - position)])
    back_phase = angles(my_slots[:, None] * all_time[None, :], length)[:, :, None]
    back_cos = jnp.cos(back_phase)
    back_sin = jnp.sin(back_phase)
    turned_real = back_real * back_cos - back_imag * back_sin
    turned_imag = back_real * back_sin + back_imag * back_cos
    inverse_scale = 1.0 / length
    gathered = lax.all_to_all(
        jnp.stack([turned_real, turned_imag]), "seq", split_axis=2, concat_axis=1, tiled=True
    )
    convolved = (
        contract("jd,jmc->dmc", block_cos, gathered[0])
        - contract("jd,jmc->dmc", block_sin, gathered[1])
    ) * inverse_scale
    returned = lax.all_to_all(
        lax.all_to_all(
            convolved.reshape(seq_count, 1, group_count, per_peer, columns),
            "seq",
            split_axis=0,
            concat_axis=1,
            tiled=True,
        ),
        "ch",
        split_axis=2,
        concat_axis=4,
        tiled=True,
    )
    convolved_rows = returned.reshape(row_count, full_width)
    gated = query_rows.astype(jnp.float32) * (convolved_rows + skip_gain[None, :] * signal)
    return gated.astype(jnp.bfloat16)


def solution(mesh):
    in_specs = (
        P(("seq", "ch"), None),
        P(("seq", "ch"), None),
        P(("seq", "ch"), None),
        P(("seq", "ch"), None),
        P(),
    )
    out_specs = P(("seq", "ch"), None)
    return jax.shard_map(shards, mesh=mesh, in_specs=in_specs, out_specs=out_specs, check_vma=False)
```

profile of v0, /device:TPU:0, one launch (start us, length us, event | category | flops | bytes accessed | tf_op | source)
XLA Modules:
  0.0 577.8 jit_solution(11160475574549039905)
XLA Ops:
  0.0 7.4 %all-to-all-start.3 = ((f32[1,8,1,8,4096]{4,3,2,0,1:T(8,128)}), f32[1,8,1,8,4096]{4,3,2,0,1:T(8,128)S(1)}, u32[]{:S(2)}, u32[]{:S(2)}) async-start(f32[1,8,1,8,4096]{4,3,2,0,1:T(8,128)} %bitcast.167), calls=%async_computation.3 | async-start | bytes 2097152 | tf_op jit(solution)/shard_map/all_to_all | solution.py:42
  7.4 1.1 fusion.15
  8.5 24.7 %all-to-all-done.3 = f32[1,8,1,8,4096]{4,3,2,0,1:T(8,128)S(1)} async-done(((f32[1,8,1,8,4096]{4,3,2,0,1:T(8,128)}), f32[1,8,1,8,4096]{4,3,2,0,1:T(8,128)S(1)}, u32[]{:S(2)}, u32[]{:S(2)}) %all-to-all-start.3) | async-done | bytes 1048608 | tf_op jit(solution)/shard_map/all_to_all | solution.py:42
  33.2 3.6 all-to-all-start
  36.8 8.7 %copy.61 = f32[8,1,1,8,4096]{3,0,2,1,4:T(8,128)} copy(f32[8,1,1,8,4096]{4,3,0,2,1:T(8,128)S(1)} %bitcast.159) | data formatting | bytes 2097152 | tf_op jit(solution)/shard_map/all_to_all | solution.py:42
  45.5 11.9 %reshape.292 = f32[4,1,65536]{2,1,0:T(1,128)} reshape(f32[4096,1,1,8,8]{4,3,2,1,0:T(8,128)} %bitcast.139) | data formatting | bytes 2097152
  57.4 5.3 all-to-all-done
  62.7 3.5 all-to-all-start.4
  66.3 8.7 %copy.52 = f32[8,1,1,8,4096]{3,0,2,1,4:T(8,128)} copy(f32[8,1,1,8,4096]{4,3,0,2,1:T(8,128)S(1)} %bitcast.158) | data formatting | bytes 2097152 | tf_op jit(solution)/shard_map/all_to_all | solution.py:35
  75.0 11.9 %reshape.290 = f32[4,1,65536]{2,1,0:T(1,128)} reshape(f32[4096,1,1,8,8]{4,3,2,1,0:T(8,128)} %bitcast.140) | data formatting | bytes 2097152
  86.9 4.7 all-to-all-start.1
  92.3 3.7 reduce
  96.0 14.8 %reshape.293 = f32[4096,1,1,8,8]{4,3,2,1,0:T(8,128)} reshape(f32[4,65536]{1,0:T(4,128)S(1)} %reduce) | data formatting | bytes 2097152
  110.8 10.0 %copy.90 = f32[8,1,1,8,4,1024]{5,4,3,0,2,1:T(4,128)S(1)} copy(f32[8,1,1,8,4,1024]{3,0,5,4,2,1:T(8,128)} %bitcast.141) | data formatting | bytes 2097152 | tf_op jit(solution)/shard_map/all_to_all | solution.py:41
  120.8 0.6 copy.63
  121.4 1.9 fusion.62
  123.3 3.2 fusion.68
  126.6 4.6 reduce.1
  131.2 15.0 %reshape.291 = f32[4096,1,1,8,8]{4,3,2,1,0:T(8,128)} reshape(f32[4,65536]{1,0:T(4,128)S(1)} %reduce.1) | data formatting | bytes 2097152
  146.2 9.8 %copy.89 = f32[8,1,1,8,4,1024]{5,4,3,0,2,1:T(4,128)S(1)} copy(f32[8,1,1,8,4,1024]{3,0,5,4,2,1:T(8,128)} %bitcast.142) | data formatting | bytes 2097152 | tf_op jit(solution)/shard_map/all_to_all | solution.py:34
  156.0 0.6 copy.54
  156.7 1.9 fusion.64
  158.6 4.8 subtract_bitcast_fusion.1
  164.0 4.4 copy.64
  168.4 4.7 all-to-all-start.5
  173.1 2.0 pad_maximum_fusion
  175.1 4.4 copy.55
  179.6 87.6 %all-to-all-done.5 = f32[2,16,32,1024]{3,2,0,1:T(8,128)} async-done(((f32[2,16,32,1024]{3,2,0,1:T(8,128)}), f32[2,16,32,1024]{3,2,0,1:T(8,128)}, u32[]{:S(2)}, u32[]{:S(2)}) %all-to-all-start.5) | async-done | bytes 4194336 | tf_op jit(solution)/shard_map/all_to_all | solution.py:101
  267.2 5.0 all-to-all-start.2
  272.4 2.5 copy.65
  274.9 0.6 fusion.169
  276.0 4.4 fusion.31
  280.5 5.8 %fusion.27 = f32[2,1024,256]{2,1,0:T(8,128)} fusion(f32[2,256,1024]{2,1,0:T(8,128)S(1)} %bitcast.145, s32[256]{0:T(256)S(1)} %fusion.88), kind=kOutput, calls=%fused_computation.45 | convolution fusion | flops 1611530240 | bytes 4195328 | tf_op jit(solution)/shard_map/qp,jpc->jqc/dot_general | solution.py:15
  286.3 6.0 %convolution_add_fusion = f32[2,1024,256]{2,1,0:T(8,128)} fusion(f32[2,1024,256]{2,1,0:T(8,128)S(1)} %fusion.31, f32[2,256,1024]{2,1,0:T(8,128)S(1)} %bitcast.146, s32[256]{0:T(256)S(1)} %fusion.88), kind=kOutput, calls=%fused_computation.23 | convolution fusion | flops 1612054528 | bytes 6292480 | tf_op jit(solution)/shard_map/qp,jpc->jqc/dot_general | solution.py:15
  292.3 72.9 %all-to-all-done.2 = f32[2,16,32,1024]{3,2,0,1:T(8,128)} async-done(((f32[2,16,32,1024]{3,2,0,1:T(8,128)}), f32[2,16,32,1024]{3,2,0,1:T(8,128)}, u32[]{:S(2)}, u32[]{:S(2)}) %all-to-all-start.2) | async-done | bytes 4194336 | tf_op jit(solution)/shard_map/all_to_all | solution.py:98
  365.1 2.5 copy.56
  367.6 0.6 fusion.170
  368.5 4.4 fusion.33
  373.1 4.5 fusion.29
  377.6 4.7 convolution_add_fusion.1
  382.4 4.3 convolution_subtract_fusion
  386.7 5.0 multiply_subtract_fusion
  391.7 2.8 fusion.2
  394.6 2.8 fusion
  397.4 2.8 fusion.8
  400.3 3.4 subtract_bitcast_fusion
  403.6 2.2 pad_maximum_fusion.2
  405.8 7.4 %copy.74 = f32[2,2,256,1024]{3,1,0,2:T(2,128)} copy(f32[2,2,256,1024]{2,3,1,0:T(8,128)} %pad_maximum_fusion.2) | data formatting | bytes 8388608 | tf_op jit(solution)/shard_map/stack | solution.py:123
  413.3 96.9 %all_to_all.126 = f32[2,2,256,1024]{3,1,0,2:T(2,128)S(1)} all-to-all(f32[2,2,256,1024]{3,1,0,2:T(2,128)} %copy.74), channel_id=1, replica_groups=mesh['seq'=8,'ch'=4] {'seq'}, dimensions={2} | all-to-all | bytes 8388608 | tf_op jit(solution)/shard_map/all_to_all | solution.py:122
  510.2 2.4 copy.75
  512.6 1.8 fusion.168
  514.4 1.6 copy.76
  516.0 2.4 squeeze.22
  518.5 2.9 fusion.66
  521.4 3.0 copy.77
  524.3 2.7 squeeze.23
  527.0 1.1 fusion.14
  528.2 0.6 copy.78
  528.8 28.9 %all_to_all.127 = f32[8,1,4,8,1024]{4,3,2,1,0:T(8,128)S(1)} all-to-all(f32[8,1,4,8,1024]{4,3,2,1,0:T(8,128)S(1)} %copy.78), channel_id=1, replica_groups=mesh['seq'=8,'ch'=4] {'seq'}, dimensions={0} | all-to-all | bytes 2097152 | tf_op jit(solution)/shard_map/all_to_all | solution.py:130
  557.7 0.6 copy.79
  558.3 16.9 %all_to_all.128 = f32[1,8,4,8,1024]{4,1,3,0,2:T(8,128)S(1)} all-to-all(f32[1,8,4,8,1024]{4,1,3,0,2:T(8,128)S(1)} %copy.79), channel_id=1, replica_groups=mesh['seq'=8,'ch'=4] {'ch'}, dimensions={2} | all-to-all | bytes 2097152 | tf_op jit(solution)/shard_map/all_to_all | solution.py:129
  575.2 0.7 copy.93
  575.9 0.6 copy.91
  576.5 1.1 multiply_convert_fusion
  (36 shorter events, 2.5 us)
Async XLA Ops:
  0.0 7.4 %copy-start.7 = (bf16[64,4096]{1,0:T(8,128)(2,1)S(1)}, bf16[64,4096]{1,0:T(8,128)(2,1)}, u32[]{:S(2)}) copy-start(bf16[64,4096]{1,0:T(8,128)(2,1)} %param.6) | copy-start | bytes 1572868
  0.0 7.4 %copy-start.5 = (bf16[64,4096]{1,0:T(8,128)(2,1)S(1)}, bf16[64,4096]{1,0:T(8,128)(2,1)}, u32[]{:S(2)}) copy-start(bf16[64,4096]{1,0:T(8,128)(2,1)} %param.7) | copy-start | bytes 1572868
  0.0 33.2 %all-to-all-start.3 = ((f32[1,8,1,8,4096]{4,3,2,0,1:T(8,128)}), f32[1,8,1,8,4096]{4,3,2,0,1:T(8,128)S(1)}, u32[]{:S(2)}, u32[]{:S(2)}) async-start(f32[1,8,1,8,4096]{4,3,2,0,1:T(8,128)} %bitcast.167), calls=%async_computation.3 | async-start | bytes 2097152 | tf_op jit(solution)/shard_map/all_to_all | solution.py:42
  33.2 29.5 %all-to-all-start = ((f32[1,8,1,8,4096]{4,3,2,0,1:T(8,128)}), f32[1,8,1,8,4096]{4,3,2,0,1:T(8,128)S(1)}, u32[]{:S(2)}, u32[]{:S(2)}) async-start(f32[1,8,1,8,4096]{4,3,2,0,1:T(8,128)} %fusion.15), calls=%async_computation | async-start | bytes 2097152 | tf_op jit(solution)/shard_map/all_to_all | solution.py:35
  62.7 24.2 %all-to-all-start.4 = ((f32[4,1,65536]{2,1,0:T(1,128)}), f32[4,1,65536]{2,1,0:T(1,128)S(1)}, u32[]{:S(2)}, u32[]{:S(2)}) async-start(f32[4,1,65536]{2,1,0:T(1,128)} %reshape.292), calls=%async_computation.4 | async-start | bytes 2097152 | tf_op jit(solution)/shard_map/all_to_all | solution.py:41
  86.9 39.6 %all-to-all-start.1 = ((f32[4,1,65536]{2,1,0:T(1,128)}), f32[4,1,65536]{2,1,0:T(1,128)}, u32[]{:S(2)}, u32[]{:S(2)}) async-start(f32[4,1,65536]{2,1,0:T(1,128)} %reshape.290), calls=%async_computation.1 | async-start | bytes 2097152 | tf_op jit(solution)/shard_map/all_to_all | solution.py:34
  156.6 1.9 copy-start
  168.4 4.7 copy-start.2
  168.4 98.8 %all-to-all-start.5 = ((f32[2,16,32,1024]{3,2,0,1:T(8,128)}), f32[2,16,32,1024]{3,2,0,1:T(8,128)}, u32[]{:S(2)}, u32[]{:S(2)}) async-start(f32[2,16,32,1024]{3,2,0,1:T(8,128)} %copy.64), calls=%async_computation.5 | async-start | bytes 8388608 | tf_op jit(solution)/shard_map/all_to_all | solution.py:101
  267.2 97.9 %all-to-all-start.2 = ((f32[2,16,32,1024]{3,2,0,1:T(8,128)}), f32[2,16,32,1024]{3,2,0,1:T(8,128)}, u32[]{:S(2)}, u32[]{:S(2)}) async-start(f32[2,16,32,1024]{3,2,0,1:T(8,128)} %copy.55), calls=%async_computation.2 | async-start | bytes 8388608 | tf_op jit(solution)/shard_map/all_to_all | solution.py:98
  377.6 4.7 copy-start.1
  382.4 4.3 copy-start.4
  518.5 2.9 copy-start.3
  575.2 1.3 copy-start.6
  575.2 1.3 copy-start.8
  575.2 1.4 copy-start.9
  575.2 1.4 copy-start.10
where the time goes:
time: 584 us; the launch traced here: 578 us
  waiting for transfers between devices  190 us (33%)
  blocking collectives  143 us (24%)
  local copies, waits for them, and re-layouts  133 us (23%)
  matrix products  66.9 us (11%)
  starting transfers between devices  28.9 us (5%)
  other arithmetic  15.6 us (3%)
    all_to_all x1, blocking collectives, shards(): lax.all_to_all(jnp.stack([turned_real, turned_imag]), 'seq', split_axis=2...  96.9 us
    all_to_all x1, waiting for transfers between devices, shards(): lax.all_to_all(forward_blocks(moved_filter), 'seq', split_axis=1, concat_...  87.6 us
    all_to_all x1, waiting for transfers between devices, shards(): lax.all_to_all(forward_blocks(moved_signal), 'seq', split_axis=1, concat_...  72.9 us
    dot_general x18, matrix products, contract(): jnp.einsum(pattern, weights, operand, precision=highest, preferred_elemen...  66.9 us
    unnamed x27, local copies, waits for them, and re-layouts  54.3 us
    all_to_all x1, blocking collectives, shards(): lax.all_to_all(convolved.reshape(seq_count, 1, group_count, per_peer, col...  28.9 us
    all_to_all x1, waiting for transfers between devices, shards(): lax.all_to_all(filter_taps.reshape(layout), 'seq', split_axis=1, concat_a...  24.7 us
    all_to_all x1, blocking collectives, shards(): lax.all_to_all(lax.all_to_all(convolved.reshape(seq_count, 1, group_count...  16.9 us
  transfers between devices with their start and end apart: 6, of which 4 were waited for; matrix products, arithmetic and copies ran while one was open for 18% of the time, Pallas kernels for 0%

commit v1 on v0

--- a/solution.py
+++ b/solution.py
@@ -5,6 +5,22 @@
 from jax.sharding import PartitionSpec as P
 
 highest = lax.Precision.HIGHEST
+
+
+def swapped_with_each(value, axis, split, join):
+    ways, here = (lax.axis_size(axis), lax.axis_index(axis))
+    width = value.shape[split] // ways
+    dims = list(value.shape)
+    dims[split] = width
+    height = dims[join]
+    dims[join] = height * ways
+    full = jnp.zeros(dims, value.dtype)
+    for mask in range(ways):
+        part = lax.dynamic_slice_in_dim(value, (here ^ mask) * width, width, axis=split)
+        if mask:
+            part = lax.ppermute(part, axis, [(d, d ^ mask) for d in range(ways)])
+        full = lax.dynamic_update_slice_in_dim(full, part, (here ^ mask) * height, axis=join)
+    return full
 
 
 def angles(product_ids, modulus):
@@ -38,14 +54,13 @@
             concat_axis=2,
             tiled=True,
         ),
-        lax.all_to_all(
+        swapped_with_each(
             lax.all_to_all(
                 filter_taps.reshape(layout), "seq", split_axis=1, concat_axis=0, tiled=True
             ),
             "ch",
-            split_axis=4,
-            concat_axis=2,
-            tiled=True,
+            4,
+            2,
         ),
     )
     moved_signal = moved_signal.reshape(seq_count, local_rows, columns)

time: 584 us -> 565 us (0.967)
  local copies, waits for them, and re-layouts: 133 us -> 91.4 us
  waiting for transfers between devices: 190 us -> 219 us
    unnamed x27 -> x23, local copies, waits for them, and re-layouts: 54.3 us -> 29.4 us
    all_to_all x4 -> x0, local copies, waits for them, and re-layouts: 19.9 us -> none  [the longest x3 11.1 us: shards(): lax.all_to_all(lax.all_to_all(filter_taps.reshape(layout), 'seq', split_a...]
    all_to_all x1, waiting for transfers between devices: 5.3 us -> 23.6 us  [shards(): lax.all_to_all(signal.reshape(layout), 'seq', split_axis=1, concat_axis=0...]
    all_to_all x1, waiting for transfers between devices: 0.01 us -> 11.8 us  [shards(): lax.all_to_all(lax.all_to_all(signal.reshape(layout), 'seq', split_axis=1...]
    all_to_all x2 -> x3, local copies, waits for them, and re-layouts: 10.5 us -> 13.1 us  [shards(): lax.all_to_all(lax.all_to_all(signal.reshape(layout), 'seq', split_axis=1...]
  transfers between devices with their start and end apart: 6 -> 8, of which waited for: 4 -> 5; matrix products, arithmetic and copies ran while one was open for 18% -> 9% of each run, Pallas kernels for 0% -> 0%
where the time goes in v1:
time: 565 us; the launch traced here: 560 us
  waiting for transfers between devices  219 us (39%)
  blocking collectives  143 us (25%)
  local copies, waits for them, and re-layouts  91.4 us (16%)
  matrix products  66.6 us (12%)
  starting transfers between devices  27.2 us (5%)
  other arithmetic  12.9 us (2%)
    all_to_all x1, blocking collectives, shards(): lax.all_to_all(jnp.stack([turned_real, turned_imag]), 'seq', split_axis=2...  96.9 us
    all_to_all x1, waiting for transfers between devices, shards(): lax.all_to_all(forward_blocks(moved_filter), 'seq', split_axis=1, concat_...  86.8 us
    all_to_all x1, waiting for transfers between devices, shards(): lax.all_to_all(forward_blocks(moved_signal), 'seq', split_axis=1, concat_...  71.9 us
    dot_general x18, matrix products, contract(): jnp.einsum(pattern, weights, operand, precision=highest, preferred_elemen...  66.6 us
    unnamed x23, local copies, waits for them, and re-layouts  29.4 us
    all_to_all x1, blocking collectives, shards(): lax.all_to_all(convolved.reshape(seq_count, 1, group_count, per_peer, col...  28.9 us
    all_to_all x1, waiting for transfers between devices, shards(): lax.all_to_all(filter_taps.reshape(layout), 'seq', split_axis=1, concat_a...  24.7 us
    all_to_all x1, waiting for transfers between devices, shards(): lax.all_to_all(signal.reshape(layout), 'seq', split_axis=1, concat_axis=0...  23.6 us
  transfers between devices with their start and end apart: 8, of which 5 were waited for; matrix products, arithmetic and copies ran while one was open for 9% of the time, Pallas kernels for 0%

profile of v1, /device:TPU:0, one launch (start us, length us, event | category | flops | bytes accessed | tf_op | source)
XLA Modules:
  0.0 560.2 jit_solution(16858539066623607611)
XLA Ops:
  0.0 7.4 %all-to-all-start.3 = ((f32[1,8,1,8,4096]{4,3,2,0,1:T(8,128)}), f32[1,8,1,8,4096]{4,3,2,0,1:T(8,128)S(1)}, u32[]{:S(2)}, u32[]{:S(2)}) async-start(f32[1,8,1,8,4096]{4,3,2,0,1:T(8,128)} %bitcast.171), calls=%async_computation.3 | async-start | bytes 2097152 | tf_op jit(solution)/shard_map/all_to_all | solution.py:58
  7.4 1.1 fusion.15
  8.5 24.7 %all-to-all-done.3 = f32[1,8,1,8,4096]{4,3,2,0,1:T(8,128)S(1)} async-done(((f32[1,8,1,8,4096]{4,3,2,0,1:T(8,128)}), f32[1,8,1,8,4096]{4,3,2,0,1:T(8,128)S(1)}, u32[]{:S(2)}, u32[]{:S(2)}) %all-to-all-start.3) | async-done | bytes 1048608 | tf_op jit(solution)/shard_map/all_to_all | solution.py:58
  33.2 3.6 all-to-all-start
  37.2 1.6 collective-permute-start.1
  38.7 0.4 collective-permute-start.2
  39.1 23.6 %all-to-all-done = f32[1,8,1,8,4096]{4,3,2,0,1:T(8,128)S(1)} async-done(((f32[1,8,1,8,4096]{4,3,2,0,1:T(8,128)}), f32[1,8,1,8,4096]{4,3,2,0,1:T(8,128)S(1)}, u32[]{:S(2)}, u32[]{:S(2)}) %all-to-all-start) | async-done | bytes 1048608 | tf_op jit(solution)/shard_map/all_to_all | solution.py:51
  62.7 8.8 %copy.60 = f32[8,1,1,8,4096]{3,0,2,1,4:T(8,128)} copy(f32[8,1,1,8,4096]{4,3,0,2,1:T(8,128)S(1)} %bitcast.163) | data formatting | bytes 2097152 | tf_op jit(solution)/shard_map/all_to_all | solution.py:51
  71.5 11.9 %reshape.295 = f32[4,1,65536]{2,1,0:T(1,128)} reshape(f32[4096,1,1,8,8]{4,3,2,1,0:T(8,128)} %bitcast.146) | data formatting | bytes 2097152
  83.4 4.4 all-to-all-start.1
  88.7 1.9 fusion.62
  90.6 11.8 %all-to-all-done.1 = f32[4,1,65536]{2,1,0:T(1,128)} async-done(((f32[4,1,65536]{2,1,0:T(1,128)}), f32[4,1,65536]{2,1,0:T(1,128)}, u32[]{:S(2)}, u32[]{:S(2)}) %all-to-all-start.1) | async-done | bytes 1048608 | tf_op jit(solution)/shard_map/all_to_all | solution.py:50
  102.3 0.5 broadcast.519
  102.8 5.5 reduce
  108.3 16.8 %reshape.296 = f32[4096,1,1,8,8]{4,3,2,1,0:T(8,128)} reshape(f32[4,65536]{1,0:T(4,128)} %reduce) | data formatting | bytes 2097152
  125.2 10.8 %copy.102 = f32[8,1,1,8,4,1024]{5,4,3,0,2,1:T(4,128)} copy(f32[8,1,1,8,4,1024]{3,0,5,4,2,1:T(8,128)} %bitcast.147) | data formatting | bytes 2097152 | tf_op jit(solution)/shard_map/all_to_all | solution.py:50
  136.0 1.8 copy.62
  137.8 1.9 fusion.64
  139.7 1.9 fusion.70
  141.6 5.9 %subtract_bitcast_fusion.1 = (f32[1,16,32,1024]{3,1,2,0:T(8,128)S(1)}, f32[1,16,32,1024]{3,1,2,0:T(8,128)S(1)}, f32[1,16,32,1024]{3,1,2,0:T(8,128)}, f32[1,16,32,1024]{3,1,2,0:T(8,128)}) fusion(f32[16,32,1024]{2,0,1:T(8,128)S(1)} %fusion.62, f32[16,32]{0,1:T(8,128)S(1)} %get-tuple-element.28, f32[16,32]{0,1:T(8,128)S(1)} %get-tuple-element.27, ...), kind=kOutput, calls=%fused_computation.16 | convolution fusion | flops 57673472 | bytes 15732800 | tf_op jit(solution)/shard_map/jd,dmc->jmc/dot_general | solution.py:31
  147.4 0.6 pad_maximum_fusion.1
  148.0 4.4 copy.77
  152.4 4.7 all-to-all-start.4
  157.2 2.0 pad_maximum_fusion
  159.2 4.5 copy.63
  163.6 86.8 %all-to-all-done.4 = f32[2,16,32,1024]{3,2,0,1:T(8,128)} async-done(((f32[2,16,32,1024]{3,2,0,1:T(8,128)}), f32[2,16,32,1024]{3,2,0,1:T(8,128)}, u32[]{:S(2)}, u32[]{:S(2)}) %all-to-all-start.4) | async-done | bytes 4194336 | tf_op jit(solution)/shard_map/all_to_all | solution.py:116
  250.4 5.1 all-to-all-start.2
  255.7 2.5 copy.78
  258.2 0.6 fusion.169
  258.8 0.2 copy.79
  259.1 0.2 copy.81
  259.3 4.4 fusion.31
  263.7 5.8 %fusion.27 = f32[2,1024,256]{2,1,0:T(8,128)} fusion(f32[2,256,1024]{2,1,0:T(8,128)S(1)} %bitcast.150, s32[256]{0:T(256)S(1)} %fusion.106), kind=kOutput, calls=%fused_computation.45 | convolution fusion | flops 1611530240 | bytes 4195328 | tf_op jit(solution)/shard_map/qp,jpc->jqc/dot_general | solution.py:31
  269.5 6.0 %convolution_add_fusion = f32[2,1024,256]{2,1,0:T(8,128)} fusion(f32[2,1024,256]{2,1,0:T(8,128)S(1)} %fusion.31, f32[2,256,1024]{2,1,0:T(8,128)S(1)} %bitcast.151, s32[256]{0:T(256)S(1)} %fusion.106), kind=kOutput, calls=%fused_computation.23 | convolution fusion | flops 1612054528 | bytes 6292480 | tf_op jit(solution)/shard_map/qp,jpc->jqc/dot_general | solution.py:31
  275.6 71.9 %all-to-all-done.2 = f32[2,16,32,1024]{3,2,0,1:T(8,128)} async-done(((f32[2,16,32,1024]{3,2,0,1:T(8,128)}), f32[2,16,32,1024]{3,2,0,1:T(8,128)}, u32[]{:S(2)}, u32[]{:S(2)}) %all-to-all-start.2) | async-done | bytes 4194336 | tf_op jit(solution)/shard_map/all_to_all | solution.py:113
  347.5 2.5 copy.64
  350.0 0.6 fusion.170
  350.8 4.4 fusion.33
  355.5 4.5 fusion.29
  360.0 4.7 convolution_add_fusion.1
  364.7 4.3 convolution_subtract_fusion
  369.1 5.0 multiply_subtract_fusion
  374.1 2.8 fusion.2
  376.9 2.8 fusion
  379.8 2.9 fusion.8
  382.7 3.3 subtract_bitcast_fusion
  386.1 2.2 pad_maximum_fusion.2
  388.3 7.4 %copy.87 = f32[2,2,256,1024]{3,1,0,2:T(2,128)} copy(f32[2,2,256,1024]{2,3,1,0:T(8,128)} %pad_maximum_fusion.2) | data formatting | bytes 8388608 | tf_op jit(solution)/shard_map/stack | solution.py:138
  395.7 96.9 %all_to_all.108 = f32[2,2,256,1024]{3,1,0,2:T(2,128)S(1)} all-to-all(f32[2,2,256,1024]{3,1,0,2:T(2,128)} %copy.87), channel_id=1, replica_groups=mesh['seq'=8,'ch'=4] {'seq'}, dimensions={2} | all-to-all | bytes 8388608 | tf_op jit(solution)/shard_map/all_to_all | solution.py:137
  492.7 2.4 copy.88
  495.1 1.8 fusion.168
  496.9 1.6 copy.89
  498.5 2.4 squeeze.22
  500.9 2.9 fusion.66
  503.8 3.0 copy.90
  506.8 2.7 squeeze.23
  509.5 1.1 fusion.14
  510.6 0.6 copy.91
  511.2 28.9 %all_to_all.109 = f32[8,1,4,8,1024]{4,3,2,1,0:T(8,128)S(1)} all-to-all(f32[8,1,4,8,1024]{4,3,2,1,0:T(8,128)S(1)} %copy.91), channel_id=1, replica_groups=mesh['seq'=8,'ch'=4] {'seq'}, dimensions={0} | all-to-all | bytes 2097152 | tf_op jit(solution)/shard_map/all_to_all | solution.py:145
  540.1 0.6 copy.92
  540.8 16.9 %all_to_all.110 = f32[1,8,4,8,1024]{4,1,3,0,2:T(8,128)S(1)} all-to-all(f32[1,8,4,8,1024]{4,1,3,0,2:T(8,128)S(1)} %copy.92), channel_id=1, replica_groups=mesh['seq'=8,'ch'=4] {'ch'}, dimensions={2} | all-to-all | bytes 2097152 | tf_op jit(solution)/shard_map/all_to_all | solution.py:144
  557.6 0.7 copy.109
  558.3 0.6 copy.103
  559.0 1.1 multiply_convert_fusion
  (38 shorter events, 1.9 us)
Async XLA Ops:
  0.0 7.4 %copy-start.6 = (bf16[64,4096]{1,0:T(8,128)(2,1)S(1)}, bf16[64,4096]{1,0:T(8,128)(2,1)}, u32[]{:S(2)}) copy-start(bf16[64,4096]{1,0:T(8,128)(2,1)} %param.6) | copy-start | bytes 1572868
  0.0 7.4 %copy-start.4 = (bf16[64,4096]{1,0:T(8,128)(2,1)S(1)}, bf16[64,4096]{1,0:T(8,128)(2,1)}, u32[]{:S(2)}) copy-start(bf16[64,4096]{1,0:T(8,128)(2,1)} %param.7) | copy-start | bytes 1572868
  0.0 33.2 %all-to-all-start.3 = ((f32[1,8,1,8,4096]{4,3,2,0,1:T(8,128)}), f32[1,8,1,8,4096]{4,3,2,0,1:T(8,128)S(1)}, u32[]{:S(2)}, u32[]{:S(2)}) async-start(f32[1,8,1,8,4096]{4,3,2,0,1:T(8,128)} %bitcast.171), calls=%async_computation.3 | async-start | bytes 2097152 | tf_op jit(solution)/shard_map/all_to_all | solution.py:58
  33.2 29.5 %all-to-all-start = ((f32[1,8,1,8,4096]{4,3,2,0,1:T(8,128)}), f32[1,8,1,8,4096]{4,3,2,0,1:T(8,128)S(1)}, u32[]{:S(2)}, u32[]{:S(2)}) async-start(f32[1,8,1,8,4096]{4,3,2,0,1:T(8,128)} %fusion.15), calls=%async_computation | async-start | bytes 2097152 | tf_op jit(solution)/shard_map/all_to_all | solution.py:51
  36.9 51.2 %collective-permute-start = (f32[8,1,1,8,1024]{4,3,0,2,1:T(8,128)S(1)}, f32[8,1,1,8,1024]{4,3,0,2,1:T(8,128)S(1)}, u32[]{:S(2)}, u32[]{:S(2)}) collective-permute-start(f32[8,1,1,8,1024]{4,3,0,2,1:T(8,128)S(1)} %get-tuple-element.21), channel_id=1, source_target_pairs={{0,1},{1,0},{2,3},{3,2},{4,5},{5,4},{6,7},{7,6},{8,9},{9,8},{10,11... | collective-permute-start | bytes 786440 | tf_op jit(solution)/shard_map/ppermute | solution.py:21
  37.2 51.1 %collective-permute-start.1 = (f32[8,1,1,8,1024]{4,3,0,2,1:T(8,128)S(1)}, f32[8,1,1,8,1024]{4,3,0,2,1:T(8,128)S(1)}, u32[]{:S(2)}, u32[]{:S(2)}) collective-permute-start(f32[8,1,1,8,1024]{4,3,0,2,1:T(8,128)S(1)} %get-tuple-element.20), channel_id=1, source_target_pairs={{0,2},{1,3},{2,0},{3,1},{4,6},{5,7},{6,4},{7,5},{8,10},{9,11},{10,... | collective-permute-start | bytes 786440 | tf_op jit(solution)/shard_map/ppermute | solution.py:21
  38.7 49.7 %collective-permute-start.2 = (f32[8,1,1,8,1024]{4,3,0,2,1:T(8,128)S(1)}, f32[8,1,1,8,1024]{4,3,0,2,1:T(8,128)S(1)}, u32[]{:S(2)}, u32[]{:S(2)}) collective-permute-start(f32[8,1,1,8,1024]{4,3,0,2,1:T(8,128)S(1)} %get-tuple-element.19), channel_id=1, source_target_pairs={{0,3},{1,2},{2,1},{3,0},{4,7},{5,6},{6,5},{7,4},{8,11},{9,10},{10,... | collective-permute-start | bytes 786440 | tf_op jit(solution)/shard_map/ppermute | solution.py:21
  83.4 18.9 %all-to-all-start.1 = ((f32[4,1,65536]{2,1,0:T(1,128)}), f32[4,1,65536]{2,1,0:T(1,128)}, u32[]{:S(2)}, u32[]{:S(2)}) async-start(f32[4,1,65536]{2,1,0:T(1,128)} %reshape.295), calls=%async_computation.1 | async-start | bytes 2097152 | tf_op jit(solution)/shard_map/all_to_all | solution.py:50
  152.4 4.7 copy-start.1
  152.4 98.0 %all-to-all-start.4 = ((f32[2,16,32,1024]{3,2,0,1:T(8,128)}), f32[2,16,32,1024]{3,2,0,1:T(8,128)}, u32[]{:S(2)}, u32[]{:S(2)}) async-start(f32[2,16,32,1024]{3,2,0,1:T(8,128)} %copy.77), calls=%async_computation.4 | async-start | bytes 8388608 | tf_op jit(solution)/shard_map/all_to_all | solution.py:116
  250.4 97.1 %all-to-all-start.2 = ((f32[2,16,32,1024]{3,2,0,1:T(8,128)}), f32[2,16,32,1024]{3,2,0,1:T(8,128)}, u32[]{:S(2)}, u32[]{:S(2)}) async-start(f32[2,16,32,1024]{3,2,0,1:T(8,128)} %copy.63), calls=%async_computation.2 | async-start | bytes 8388608 | tf_op jit(solution)/shard_map/all_to_all | solution.py:113
  360.0 4.7 copy-start
  364.7 4.3 copy-start.3
  500.9 2.9 copy-start.2
  557.6 1.3 copy-start.5
  557.6 1.3 copy-start.7
  557.6 1.4 copy-start.8
  557.6 1.4 copy-start.9
